TPU v7x, 512 devices: a whole 4x8x8 slice. The times are simulated.
512 devices in a mesh: row: 8 (over y), col: 8 (over z_hi, x), depth: 8 (over z_lo, core).
Axes of the slice: x: 4, y: 8, z: 8 (z_hi: 2, z_lo: 4; z = z_hi * 4 + z_lo), core: 2. Of those that a mesh axis runs over, the one named last changes fastest.
Arguments:
- tokens: bfloat16 [512, 12288], P(('col', 'depth'), 'row'), may hold values from -6 to 6
- in_weight: bfloat16 [12288, 49152], P('row', ('col', 'depth')), may hold values from -0.0546875 to 0.0546875
- in_bias: bfloat16 [49152], P(('col', 'depth')), may hold values from -3 to 3
- out_weight: bfloat16 [49152, 12288], P(('col', 'depth'), 'row'), may hold values from -0.02734375 to 0.02734375
- out_bias: bfloat16 [12288], P('row'), may hold values from -3 to 3
Outputs:
- outputs: bfloat16 [512, 12288], P(('col', 'depth'), 'row')
All inputs are finite; a program needn't handle non-finite values.
Results may differ from a plain program's by a relative error of at most 0.0044.
Values may be sent and summed in bfloat16 or wider, within the bound.
A program may use at most 64 MiB of HBM per device.

v0:
```python
import jax
import jax.numpy as jnp
from jax import lax
from jax.sharding import PartitionSpec as P


def local(tokens, in_weight, in_bias, out_weight, out_bias):
    partial_pre = jnp.dot(
        lax.all_gather(tokens, ("col", "depth"), axis=0, tiled=True),
        in_weight,
        preferred_element_type=jnp.float32,
    )
    bias_wide = in_bias.astype(jnp.float32)
    share_pre = lax.psum_scatter(partial_pre, "row", scatter_dimension=0, tiled=True)
    local_hidden = jax.nn.gelu(share_pre + bias_wide, approximate=True).astype(jnp.bfloat16)
    hidden = lax.all_gather(local_hidden, "row", axis=0, tiled=True)
    summed_out = lax.psum_scatter(
        jnp.dot(hidden, out_weight, preferred_element_type=jnp.float32),
        ("col", "depth"),
        scatter_dimension=0,
        tiled=True,
    )
    return (summed_out + out_bias.astype(jnp.float32)).astype(jnp.bfloat16)


def solution(mesh):
    in_specs = (
        P(("col", "depth"), "row"),
        P("row", ("col", "depth")),
        P(("col", "depth")),
        P(("col", "depth"), "row"),
        P("row"),
    )
    out_specs = P(("col", "depth"), "row")
    return jax.shard_map(local, mesh=mesh, in_specs=in_specs, out_specs=out_specs, check_vma=False)
```

profile of v0, /device:TPU:24, one launch (start us, length us, event | category | flops | bytes accessed | tf_op | source)
XLA Modules:
  0.0 480.5 jit_solution(8272329125633772402)
XLA Ops:
  6.5 0.0 copy-start
  6.5 0.0 all-gather.2.cloned.1.call-start
  6.5 0.7 all-gather.2.cloned.1.call-update
  7.3 0.0 copy-start.2
  7.3 0.0 reduce-scatter.3.cloned.1.call-start
  7.3 123.4 %all-gather.2.cloned.1.call-done = bf16[512,1536]{1,0:T(8,128)(2,1)} async-done(((bf16[8,1536]{1,0:T(8,128)(2,1)}), bf16[512,1536]{1,0:T(8,128)(2,1)}) %all-gather.2.cloned.1.call-update) | async-done | bytes 1572880 | tf_op jit(solution)/shard_map/all_gather | solution.py:9
  130.7 4.7 fusion.8
  135.4 0.0 reduce-scatter.3.cloned.1.call-update
  135.4 0.0 reduce-scatter.5.cloned.1.call-start
  135.5 0.0 copy-done.2
  135.5 40.7 %reduce-scatter.3.cloned.1.call-done = f32[64,768]{1,0:T(8,128)} async-done(((f32[512,768]{1,0:T(8,128)}), f32[64,768]{1,0:T(8,128)}) %reduce-scatter.3.cloned.1.call-update) | async-done | bytes 196624 | tf_op jit(solution)/shard_map/reduce_scatter | solution.py:14
  176.3 1.0 fusion.7
  177.3 26.0 %all_gather.7 = bf16[512,768]{1,0:T(8,128)(2,1)S(1)} all-gather(bf16[64,768]{1,0:T(8,128)(2,1)S(1)} %fusion.7), channel_id=1, replica_groups=mesh['row'=8,'col'=8,'depth'=8] {'row'}, dimensions={0}, use_global_device_ids=true | all-gather | bytes 884736 | tf_op jit(solution)/shard_map/all_gather | solution.py:16
  203.2 0.0 copy-done
  203.2 3.0 fusion.9
  206.3 0.0 copy-start.1
  206.3 0.0 reduce-scatter.5.cloned.1.call-update
  206.3 0.7 copy-done.1
  207.0 265.6 %reduce-scatter.5.cloned.1.call-done = f32[8,1536]{1,0:T(8,128)} async-done(((f32[512,1536]{1,0:T(8,128)}), f32[8,1536]{1,0:T(8,128)}) %reduce-scatter.5.cloned.1.call-update) | async-done | bytes 49168 | tf_op jit(solution)/shard_map/reduce_scatter | solution.py:17
  472.6 1.4 add_convert_fusion
  (2 shorter events, 0.0 us)
Async XLA Ops:
  6.5 196.7 %copy-start = (bf16[768,1536]{1,0:T(8,128)(2,1)S(1)}, bf16[768,1536]{1,0:T(8,128)(2,1)}, u32[]{:S(2)}) copy-start(bf16[768,1536]{1,0:T(8,128)(2,1)} %param.8) | copy-start | bytes 7077892
  6.5 124.2 %all-gather.2.cloned.1.call-start = ((), (), s32[]{:S(2)}) async-start(), calls=%async_computation.2 | async-start | bytes 1597440 | tf_op jit(solution)/shard_map/all_gather | solution.py:9
  7.3 128.2 %copy-start.2 = (bf16[768]{0:T(1024)(128)(2,1)S(1)}, bf16[768]{0:T(1024)(128)(2,1)}, u32[]{:S(2)}) copy-start(bf16[768]{0:T(1024)(128)(2,1)} %param.7) | copy-start | bytes 4612
  7.3 169.0 %reduce-scatter.3.cloned.1.call-start = ((), (), s32[]{:S(2)}) async-start(), calls=%async_computation.3 | async-start | bytes 1769472 | tf_op jit(solution)/shard_map/reduce_scatter | solution.py:14
  135.4 337.1 %reduce-scatter.5.cloned.1.call-start = ((), (), s32[]{:S(2)}) async-start(), calls=%async_computation.4 | async-start | bytes 3194880 | tf_op jit(solution)/shard_map/reduce_scatter | solution.py:17
  206.3 0.7 copy-start.1
Sparse Core Ops, SparseCore 0:
  9.5 121.1 all-gather.1
  135.6 40.6 reduce-scatter.2
  206.4 266.0 reduce-scatter.4
where the time goes:
time: 481 us; the launch traced here: 480 us
  waiting for transfers between devices  430 us (89%)
  blocking collectives  26 us (5%)
  between operations  13.1 us (3%)
  matrix products  7.72 us (2%)
    reduce_scatter x1, waiting for transfers between devices, local(): lax.psum_scatter(jnp.dot(hidden, out_weight, preferred_element_type=jnp.f...  266 us
    all_gather x1, waiting for transfers between devices, local(): lax.all_gather(tokens, ('col', 'depth'), axis=0, tiled=True)  123 us
    reduce_scatter x1, waiting for transfers between devices, local(): lax.psum_scatter(partial_pre, 'row', scatter_dimension=0, tiled=True)  40.7 us
    all_gather x1, blocking collectives, local(): hidden = lax.all_gather(local_hidden, 'row', axis=0, tiled=True)  26 us
  transfers between devices with their start and end apart: 3, of which 3 were waited for; matrix products, arithmetic and copies ran while one was open for 0% of the time, Pallas kernels for 0%

commit v1 on v0

v1 whole, which is shorter than its diff:
```python
import jax
import jax.numpy as jnp
from jax import lax
from jax.experimental import pallas as pl
from jax.experimental.pallas import tpu as pltpu
from jax.sharding import PartitionSpec as P

BF, F32 = jnp.bfloat16, jnp.float32
H = 768
NB = 3
W = H // NB


def kernel(tok_ref, w1_ref, b1_ref, w2_ref, b2_ref, out_ref,
           w1v, w2v, tsend, trecv, tok, pm, s_a, s_b, r_a, r_b, hid, po, os_, xr, zs, zr, zown, fs, fr,
           lsem, wsem, tsem, zsem, zsend, xsem, xsend, csem, csend,
           ra_sem, rb_sem, rsend, ha_sem, hb_sem, hsend, hc_sem, hcsend,
           ox_sem, oxsend, oz_sem, ozsend, fsem):
    y = lax.axis_index("row")
    col = lax.axis_index("col")
    dep = lax.axis_index("depth")
    x = col % 4
    z = (col // 4) * 4 + dep // 2
    c = dep % 2
    sg = 1 - 2 * c

    def dev(dx=0, dy=0, dz=0, dc=0):
        px, py, pz, pc = (x + dx) % 4, (y + dy + 8) % 8, (z + dz) % 8, (c + dc) % 2
        return {"row": py, "col": (pz // 4) * 4 + px, "depth": (pz % 4) * 2 + pc}

    def send(src, dst, ssem, rsem, to):
        pltpu.make_async_remote_copy(
            src_ref=src, dst_ref=dst, send_sem=ssem, recv_sem=rsem,
            device_id=to, device_id_type=pl.DeviceIdType.MESH).start()

    def wait(ref, sem):
        pltpu.make_async_copy(ref, ref, sem).wait()

    other = dev(dc=1)
    w1_copy = pltpu.make_async_copy(w1_ref, w1v, lsem.at[0])
    w1_copy.start()
    w2_copy = pltpu.make_async_copy(
        w2_ref.at[:, pl.ds(pl.multiple_of(c * H, H), H)], w2v.at[c], lsem.at[1])
    w2_copy.start()

    barrier = pltpu.get_barrier_semaphore()
    partners = [other, dev(dy=1), dev(dy=-1)]
    partners += [dev(dx=e) for e in (1, 2, 3)] + [dev(dz=d) for d in range(1, 8)]
    for to in partners:
        pl.semaphore_signal(barrier, inc=1, device_id=to, device_id_type=pl.DeviceIdType.MESH)
    pl.semaphore_wait(barrier, len(partners))

    left = tok_ref[:, :H].astype(F32)
    right = tok_ref[:, H:].astype(F32)
    first = c == 0
    tsend[...] = jnp.where(first, right, left)
    send(tsend, trecv, tsem.at[0], tsem.at[1], other)
    send(w2_ref.at[:, pl.ds(pl.multiple_of((1 - c) * H, H), H)], w2v.at[c], wsem.at[0], wsem.at[1], other)
    mine = jnp.where(first, left, right)

    def slot_of(pz, s):
        g = (s * (pz - y) + 23) % 8
        hi = g // 4
        return (1 - hi) * (6 - 2 * g) + hi * (2 * g - 7)

    def rows_of(pz, s, n, off=0):
        return pl.ds(pl.multiple_of(slot_of(pz, s) * 64 + off, 16), n)

    wait(trecv, tsem.at[1])
    theirs = trecv[...]
    own_rows = tok.at[c, rows_of(z, sg, 16, x * 16)]
    own_rows[...] = jnp.concatenate(
        [jnp.where(first, mine, theirs), jnp.where(first, theirs, mine)], axis=0).astype(BF)

    order = (4, 3, 5, 2, 6, 1, 7)
    for d in order:
        send(own_rows, own_rows, zsend, zsem.at[d], dev(dz=d))
    for d in (0, 1, 7, 2, 6, 3, 5, 4):
        piece = tok.at[c, rows_of(z - d + 8, sg, 16, x * 16)]
        if d:
            wait(piece, zsem.at[d])
        for e in (2, 1, 3):
            send(piece, piece, xsend, xsem.at[d, e - 1], dev(dx=e))
    for d in (0, 1, 7, 2, 6, 3, 5, 4):
        for e in (1, 3, 2):
            wait(tok.at[c, rows_of(z - d + 8, sg, 16, ((x - e + 4) % 4) * 16)], xsem.at[d, e - 1])
        send(tok.at[c, rows_of(z - d + 8, sg, 64)], tok.at[c, rows_of(z - d + 8, -sg, 64)],
             csend, csem.at[d], other)
    w1_copy.wait()
    for d in range(8):
        wait(tok.at[1 - c, rows_of(z - d + 8, sg, 64)], csem.at[d])

    def product(s, cols):
        rows = slice(s * 128, s * 128 + 128)
        return (jnp.dot(tok[0, rows, :], w1v[:H, cols], preferred_element_type=F32)
                + jnp.dot(tok[1, rows, :], w1v[H:, cols], preferred_element_type=F32))

    ahead, back = dev(dy=sg), dev(dy=-sg)
    for s in range(4):
        if s:
            for n in range(NB):
                cols = slice(n * W, n * W + W)
                pm[s * 128:s * 128 + 128, cols] = product(s, cols)
        for n in range(NB):
            cols = slice(n * W, n * W + W)
            if s == 0:
                part = product(0, cols)
                part_a, part_b = part[:64], part[64:]
            else:
                wait(r_a.at[s - 1, :, cols], ra_sem.at[s - 1, n])
                part_a = pm[s * 128:s * 128 + 64, cols] + r_a[s - 1, :, cols].astype(F32)
            s_a[s, :, cols] = part_a.astype(BF)
            send(s_a.at[s, :, cols], r_a.at[s, :, cols], rsend.at[0], ra_sem.at[s, n], ahead)
            if s:
                wait(r_b.at[s - 1, :, cols], rb_sem.at[s - 1, n])
                part_b = pm[s * 128 + 64:s * 128 + 128, cols] + r_b[s - 1, :, cols].astype(F32)
            if s < 3:
                s_b[s, :, cols] = part_b.astype(BF)
                send(s_b.at[s, :, cols], r_b.at[s, :, cols], rsend.at[1], rb_sem.at[s, n], back)
            else:
                pm[448:512, cols] = part_b

    def chunk(slot, cols):
        return hid.at[c, pl.ds(pl.multiple_of(slot * 64, 64), 64), cols]

    for n in range(NB):
        cols = slice(n * W, n * W + W)
        wait(r_a.at[3, :, cols], ra_sem.at[3, n])
        v = pm[448:512, cols] + r_a[3, :, cols].astype(F32) + b1_ref[:, cols].astype(F32)
        chunk(0, cols)[...] = jax.nn.gelu(v, approximate=True).astype(BF)
        send(chunk(0, cols), chunk(2 - c, cols), hsend.at[0], ha_sem.at[0, n], ahead)
        send(chunk(0, cols), chunk(1 + c, cols), hsend.at[1], hb_sem.at[0, n], back)
        send(chunk(0, cols), chunk(0, cols), hcsend, hc_sem.at[0, n], other)

    w2_copy.wait()
    wait(w2v.at[1 - c], wsem.at[1])

    def second(slot, count):
        rows = slice(slot * 64, (slot + count) * 64)
        po[rows, :] = (jnp.dot(hid[0, rows, :], w2v[0], preferred_element_type=F32)
                       + jnp.dot(hid[1, rows, :], w2v[1], preferred_element_type=F32))
        os_[rows, :] = po[rows, :].astype(BF)
        for k in range(slot, slot + count):
            for e in (2, 1, 3):
                part = pl.ds(pl.multiple_of(k * 64 + ((x + e) % 4) * 16, 16), 16)
                send(os_.at[part], xr.at[k, e - 1], oxsend, ox_sem.at[k, e - 1], dev(dx=e))

    def arrived(slot):
        for n in range(NB):
            cols = slice(n * W, n * W + W)
            wait(hid.at[1 - c, slot * 64:slot * 64 + 64, cols], hc_sem.at[slot, n])

    rel = (0, 1, -1, 2, -2, 3, -3, 4)

    def along_z(k):
        mine = po[pl.ds(pl.multiple_of(k * 64 + x * 16, 16), 16), :]
        for e in (1, 3, 2):
            wait(xr.at[k, e - 1], ox_sem.at[k, e - 1])
            mine = mine + xr[k, e - 1].astype(F32)
        zs[k] = mine.astype(BF)
        d = (y + rel[k] - z + 16) % 8

        @pl.when(d == 0)
        def _():
            zown[...] = mine

        @pl.when(d != 0)
        def _():
            send(zs.at[k], zr.at[d], ozsend, oz_sem.at[d], dev(dz=d))

    pairs = ((0, 1), (1, 2), (3, 2), (5, 2), (7, 1))
    for j in range(1, 5):
        for n in range(NB):
            cols = slice(n * W, n * W + W)
            at = 7 if j == 4 else 2 * j - c
            wait(chunk(at, cols), ha_sem.at[j - 1, n])
            if j < 4:
                to = 7 if j == 3 else 2 * j + 2 - c
                send(chunk(at, cols), chunk(to, cols), hsend.at[0], ha_sem.at[j, n], ahead)
            send(chunk(at, cols), chunk(at, cols), hcsend, hc_sem.at[at, n], other)
            if j < 4:
                at = 2 * j - 1 + c
                wait(chunk(at, cols), hb_sem.at[j - 1, n])
                if j < 3:
                    send(chunk(at, cols), chunk(2 * j + 1 + c, cols), hsend.at[1], hb_sem.at[j, n], back)
                send(chunk(at, cols), chunk(at, cols), hcsend, hc_sem.at[at, n], other)
        slot, count = pairs[j - 1]
        for k in range(slot, slot + count):
            arrived(k)
        second(slot, count)
        if j > 1:
            slot, count = pairs[j - 2]
            for k in range(slot, slot + count):
                along_z(k)
    arrived(7)
    second(7, 1)
    for k in (5, 6, 7):
        along_z(k)

    total = zown[...]
    for d in (1, 7, 2, 6, 3, 5, 4):
        wait(zr.at[d], oz_sem.at[d])
        total = total + zr[d].astype(F32)
    fs[...] = jnp.where(first, total[8:], total[:8])
    send(fs, fr, fsem.at[0], fsem.at[1], other)
    mine = jnp.where(first, total[:8], total[8:])
    wait(fr, fsem.at[1])
    theirs = fr[...]
    out_ref[:, :H] = (jnp.where(first, mine, theirs) + b2_ref[:, :H].astype(F32)).astype(BF)
    out_ref[:, H:] = (jnp.where(first, theirs, mine) + b2_ref[:, H:].astype(F32)).astype(BF)

    wait(tsend, tsem.at[0])
    wait(w2v.at[0], wsem.at[0])
    wait(tok.at[0, :112], zsend)
    wait(tok.at[0, :384], xsend)
    wait(tok.at[0], csend)
    wait(tok.at[0, :256], rsend.at[0])
    wait(tok.at[0, :192], rsend.at[1])
    wait(tok.at[0, :256], hsend.at[0])
    wait(tok.at[0, :192], hsend.at[1])
    wait(tok.at[0], hcsend)
    wait(tok.at[0, :384], oxsend)
    wait(tok.at[0, :112], ozsend)
    wait(fs, fsem.at[0])


def local(tokens, in_weight, in_bias, out_weight, out_bias):
    vm = pl.BlockSpec(memory_space=pltpu.VMEM)
    hbm = pl.BlockSpec(memory_space=pl.ANY)
    dma = pltpu.SemaphoreType.DMA
    return pl.pallas_call(
        kernel,
        out_shape=jax.ShapeDtypeStruct((8, 2 * H), BF),
        in_specs=[vm, hbm, vm, hbm, vm],
        out_specs=vm,
        scratch_shapes=[
            pltpu.VMEM((2 * H, H), BF), pltpu.VMEM((2, H, H), BF),
            pltpu.VMEM((8, H), F32), pltpu.VMEM((8, H), F32),
            pltpu.VMEM((2, 512, H), BF), pltpu.VMEM((512, H), F32),
            pltpu.VMEM((4, 64, H), BF), pltpu.VMEM((3, 64, H), BF),
            pltpu.VMEM((4, 64, H), BF), pltpu.VMEM((3, 64, H), BF),
            pltpu.VMEM((2, 512, H), BF),
            pltpu.VMEM((512, H), F32), pltpu.VMEM((512, H), BF),
            pltpu.VMEM((8, 3, 16, H), BF), pltpu.VMEM((8, 16, H), BF),
            pltpu.VMEM((8, 16, H), BF), pltpu.VMEM((16, H), F32),
            pltpu.VMEM((8, H), F32), pltpu.VMEM((8, H), F32),
            dma((2,)), dma((2,)), dma((2,)), dma((8,)), dma, dma((8, 3)), dma, dma((8,)), dma,
            dma((4, NB)), dma((3, NB)), dma((2,)), dma((4, NB)), dma((3, NB)), dma((2,)),
            dma((8, NB)), dma, dma((8, 3)), dma, dma((8,)), dma, dma((2,)),
        ],
        compiler_params=pltpu.CompilerParams(
            collective_id=0, has_side_effects=True, vmem_limit_bytes=60 * 2**20),
    )(tokens, in_weight, in_bias.reshape(1, H), out_weight, out_bias.reshape(1, 2 * H))


def solution(mesh):
    in_specs = (
        P(("col", "depth"), "row"),
        P("row", ("col", "depth")),
        P(("col", "depth")),
        P(("col", "depth"), "row"),
        P("row"),
    )
    out_specs = P(("col", "depth"), "row")
    return jax.shard_map(local, mesh=mesh, in_specs=in_specs, out_specs=out_specs, check_vma=False)
```

time: 481 us -> 77 us (0.16)
  the two profiles are of different devices: /device:TPU:24 before, /device:TPU:33 now
where the time goes in v1:
time: 77 us; the launch traced here: 76.8 us
  Pallas kernels  72.9 us (95%)
  local copies, waits for them, and re-layouts  3.89 us (5%)
    pallas_call x1, Pallas kernels, local(): pl.pallas_call(kernel, out_shape=jax.ShapeDtypeStruct((8, 2 * H), BF), in...  72.9 us

profile of v1, /device:TPU:33, one launch (start us, length us, event | category | flops | bytes accessed | tf_op | source)
XLA Modules:
  0.0 76.8 jit_solution(12500524828032613837)
XLA Ops:
  0.0 1.3 %reshape.6.b1_ref = bf16[1,768]{1,0:T(2,128)(2,1)} reshape(bf16[768]{0:T(1024)(128)(2,1)} %param.7) | data formatting | bytes 3072 | tf_op jit(solution)/shard_map/reshape | solution.py:253
  1.3 1.3 %reshape.7.b2_ref = bf16[1,1536]{1,0:T(2,128)(2,1)} reshape(bf16[1536]{0:T(1024)(128)(2,1)} %param.9) | data formatting | bytes 6144 | tf_op jit(solution)/shard_map/reshape | solution.py:253
  2.5 72.9 %shard_map.55 = bf16[8,1536]{1,0:T(8,128)(2,1)} custom-call(bf16[8,1536]{1,0:T(8,128)(2,1)} %tok_ref.1, bf16[1536,768]{1,0:T(8,128)(2,1)} %w1_ref.1, bf16[1,768]{1,0:T(2,128)(2,1)} %reshape.6.b1_ref, bf16[768,1536]{1,0:T(8,128)(2,1)} %w2_ref.1, bf16[1,1536]{1,0:T(2,128)(2,1)} %reshape.7.b2_ref), custom_call_target="tpu_custom_call" | custom-call | tf_op jit(solution)/shard_map/pallas_call | solution.py:231
  75.4 1.3 %copy.7 = bf16[8,1536]{1,0:T(8,128)(2,1)} copy(bf16[8,1536]{1,0:T(8,128)(2,1)} %shard_map.55) | data formatting | bytes 49152
